TPU v7x, 512 devices: a whole 4x4x16 slice. The times are simulated.
512 devices in a mesh: section: 4 (over x_hi, core), expert: 16 (over z), tensor: 8 (over y, x_lo).
Axes of the slice: x: 4 (x_hi: 2, x_lo: 2; x = x_hi * 2 + x_lo), y: 4, z: 16, core: 2. Of those that a mesh axis runs over, the one named last changes fastest.
Arguments:
- tokens: bfloat16 [8192, 5120], P(('section', 'expert'), 'tensor'), may hold values from -6 to 6
- norm_gain: float32 [5120], P('tensor'), may hold values from 0.1 to 1.9
- router: bfloat16 [5120, 16], P('tensor'), may hold values from -0.078125 to 0.078125
- expert_ids: int32 [8192, 1], P(('section', 'expert')), may hold values from 0 to 15; in each aligned block of 128 rows (0 to 127, 128 to 255, ...) at most 16 rows name the same one
- gate_proj: bfloat16 [16, 5120, 4096], P('expert', None, ('section', 'tensor')), may hold values from -0.078125 to 0.078125
- up_proj: bfloat16 [16, 5120, 4096], P('expert', None, ('section', 'tensor')), may hold values from -0.078125 to 0.078125
- down_proj: bfloat16 [16, 4096, 5120], P('expert', 'section', 'tensor'), may hold values from -0.09375 to 0.09375
Outputs:
- moe_out: bfloat16 [8192, 5120], P(('section', 'expert'), 'tensor')
Inputs may be any that keep to these rules, and one draw needn't show every extreme that they name: `expert_ids`: within each aligned block of 128 tokens (the tokens of one group of devices along section and expert) no expert is named by more than 16 tokens, a bound that some block reaches.
All inputs are finite; a program needn't handle non-finite values.
Results may differ from a plain program's by a relative error of at most 0.017.
Values may be sent and summed in bfloat16 or wider, within the bound.
No kernel may reach another device: no remote copies, remote signals or barrier semaphores. Data moves between devices by JAX's collectives and lax.ppermute only.
A program may use at most 64 MiB of HBM per device.

v0:
```python
import jax
import jax.numpy as jnp
from jax import lax
from jax.sharding import PartitionSpec as P

D = 5120
EPSILON = 1e-05


def from_everyone(array, axis):
    count = lax.axis_size(axis)
    return lax.all_to_all(
        jnp.broadcast_to(array[None], (count, *array.shape)), axis, 0, 0, tiled=True
    )


def of_everyone(array, axis):
    return from_everyone(array, axis).sum(axis=0)


def joined_along(parts, dim):
    parts = jnp.moveaxis(parts, 0, dim)
    shape = parts.shape
    return parts.reshape(*shape[:dim], shape[dim] * shape[dim + 1], *shape[dim + 2 :])


def collect(array, axis, dim):
    return joined_along(from_everyone(array, axis), dim)


def in_blocks(array, dim, count):
    shape = array.shape
    parts = array.reshape(*shape[:dim], count, shape[dim] // count, *shape[dim + 1 :])
    return jnp.moveaxis(parts, dim, 0)


def summed_on_arrival(array, axis, dim):
    parts = in_blocks(array, dim, lax.axis_size(axis))
    arrived = lax.all_to_all(parts, axis, split_axis=0, concat_axis=0, tiled=True)
    return arrived.sum(axis=0)


def slot_table(expert_ids, experts, capacity):
    chosen = expert_ids[:, 0]
    member = (chosen[:, None] == jnp.arange(experts, dtype=jnp.int32)[None, :]).astype(jnp.int32)
    earlier = jnp.cumsum(member, axis=0) - member
    placed = chosen * capacity + jnp.sum(earlier * member, axis=1)
    placing = placed[:, None] == jnp.arange(experts * capacity, dtype=jnp.int32)[None, :]
    return (member, placing)


def normalize(tokens, norm_gain, squares):
    values = tokens.astype(jnp.float32)
    return (values * lax.rsqrt(squares / D + EPSILON) * norm_gain).astype(jnp.bfloat16)


def on_device(tokens, norm_gain, router, expert_ids, gate_proj, up_proj, down_proj):
    row_count = tokens.shape[0]
    experts = router.shape[1]
    capacity = 2 * row_count // experts
    values = tokens.astype(jnp.float32)
    squares = of_everyone(jnp.sum(values * values, axis=1, keepdims=True), "tensor")
    normed = normalize(tokens, norm_gain, squares)
    logits = of_everyone(jnp.dot(normed, router, preferred_element_type=jnp.float32), "tensor")
    member, placing = slot_table(expert_ids, experts, capacity)
    score = jax.nn.sigmoid(jnp.sum(jnp.where(member > 0, logits, jnp.float32(0.0)), axis=1))
    routed = (normed.astype(jnp.float32) * score[:, None]).astype(jnp.bfloat16)
    placing = placing.astype(jnp.bfloat16)
    outgoing = jnp.einsum("tc,td->cd", placing, routed, preferred_element_type=jnp.float32).astype(
        jnp.bfloat16
    )
    arrived = lax.all_to_all(outgoing, "expert", split_axis=0, concat_axis=0, tiled=True)
    gate_cols = gate_proj[0]
    up_cols = up_proj[0]
    down_rows = down_proj[0]
    widened = collect(arrived, "tensor", 1)
    piece = lax.all_gather(widened, "section", axis=0, tiled=True)
    gate = jnp.dot(piece, gate_cols, preferred_element_type=jnp.float32)
    upper = jnp.dot(piece, up_cols, preferred_element_type=jnp.float32)
    hidden = (jax.nn.silu(gate) * upper).astype(jnp.bfloat16)
    full_hidden = collect(hidden, "tensor", 1)
    summed = summed_on_arrival(
        jnp.dot(full_hidden, down_rows, preferred_element_type=jnp.float32), "section", 0
    )
    returned = lax.all_to_all(
        summed.astype(jnp.bfloat16), "expert", split_axis=0, concat_axis=0, tiled=True
    )
    result = jnp.einsum("tc,cd->td", placing, returned, preferred_element_type=jnp.float32)
    return result.astype(jnp.bfloat16)


def solution(mesh):
    in_specs = (
        P(("section", "expert"), "tensor"),
        P("tensor"),
        P("tensor", None),
        P(("section", "expert"), None),
        P("expert", None, ("section", "tensor")),
        P("expert", None, ("section", "tensor")),
        P("expert", "section", "tensor"),
    )
    out_specs = P(("section", "expert"), "tensor")
    return jax.shard_map(
        on_device, mesh=mesh, in_specs=in_specs, out_specs=out_specs, check_vma=False
    )
```

profile of v0, /device:TPU:64, one launch (start us, length us, event | category | flops | bytes accessed | tf_op | source)
XLA Modules:
  0.0 304.4 jit_solution(2847538108800103751)
XLA Ops:
  6.5 1.1 fusion.12
  7.7 0.6 broadcast_in_dim.14
  8.3 5.4 %all-to-all-start = ((f32[8,128,1]{1,2,0:T(1,128)}), f32[8,128,1]{1,2,0:T(1,128)S(1)}, u32[]{:S(2)}, u32[]{:S(2)}) async-start(f32[8,128,1]{1,2,0:T(1,128)} %broadcast_in_dim.14), calls=%async_computation | async-start | bytes 8192 | tf_op jit(solution)/shard_map/all_to_all | solution.py:12
  13.7 0.7 fusion.18
  14.4 0.2 reduce_window_sum.11
  14.6 0.8 select_reduce_fusion.1
  15.4 4.3 %all-to-all-done = f32[8,128,1]{1,2,0:T(1,128)S(1)} async-done(((f32[8,128,1]{1,2,0:T(1,128)}), f32[8,128,1]{1,2,0:T(1,128)S(1)}, u32[]{:S(2)}, u32[]{:S(2)}) %all-to-all-start) | async-done | bytes 4128 | tf_op jit(solution)/shard_map/all_to_all | solution.py:12
  19.8 1.1 fusion.19
  20.9 0.7 broadcast_in_dim.15
  21.6 3.4 %all-to-all-start.1 = ((f32[8,128,16]{1,2,0:T(8,128)}), f32[8,128,16]{1,2,0:T(8,128)S(1)}, u32[]{:S(2)}, u32[]{:S(2)}) async-start(f32[8,128,16]{1,2,0:T(8,128)} %broadcast_in_dim.15), calls=%async_computation.1 | async-start | bytes 131072 | tf_op jit(solution)/shard_map/all_to_all | solution.py:12
  25.0 0.7 fusion.22
  25.7 5.6 %all-to-all-done.1 = f32[8,128,16]{1,2,0:T(8,128)S(1)} async-done(((f32[8,128,16]{1,2,0:T(8,128)}), f32[8,128,16]{1,2,0:T(8,128)S(1)}, u32[]{:S(2)}, u32[]{:S(2)}) %all-to-all-start.1) | async-done | bytes 65568 | tf_op jit(solution)/shard_map/all_to_all | solution.py:12
  31.4 0.8 select_reduce_fusion
  32.2 1.3 convolution_convert_fusion
  33.5 32.8 %all_to_all.43 = bf16[16,16,640]{2,1,0:T(8,128)(2,1)S(1)} all-to-all(bf16[16,16,640]{2,1,0:T(8,128)(2,1)S(1)} %bitcast.37), channel_id=1, replica_groups=mesh['section'=4,'expert'=16,'tensor'=8] {'expert'}, dimensions={0} | all-to-all | bytes 655360 | tf_op jit(solution)/shard_map/all_to_all | solution.py:72
  66.3 0.2 copy.12
  66.5 0.2 broadcast_in_dim.18
  66.7 27.6 %all_to_all.44 = bf16[8,256,640]{1,2,0:T(8,128)(2,1)} all-to-all(bf16[8,256,640]{1,2,0:T(8,128)(2,1)S(1)} %broadcast_in_dim.18), channel_id=1, replica_groups=mesh['section'=4,'expert'=16,'tensor'=8] {'tensor'}, dimensions={0} | all-to-all | bytes 5242880 | tf_op jit(solution)/shard_map/all_to_all | solution.py:12
  94.3 82.6 %all-gather.2.cloned.1.call-done = bf16[1024,5120]{0,1:T(8,128)(2,1)} async-done(((bf16[256,5120]{0,1:T(8,128)(2,1)}), bf16[1024,5120]{0,1:T(8,128)(2,1)}) %all-gather.2.cloned.1.call-update) | async-done | bytes 10485776 | tf_op jit(solution)/shard_map/all_gather | solution.py:77
  176.8 5.8 %fusion.4 = f32[1024,128]{1,0:T(8,128)S(1)} fusion(bf16[1024,5120]{0,1:T(8,128)(2,1)} %all-gather.2.cloned.1.call-done, bf16[1,5120,128]{2,1,0:T(8,128)(2,1)S(1)} %copy-done.2), kind=kOutput, calls=%fused_computation.4 | convolution fusion | flops 1342177280 | bytes 12320768 | tf_op jit(solution)/shard_map/dot_general | solution.py:78
  182.7 1.2 copy-done.1
  183.9 0.3 copy-done.3
  184.2 2.9 fusion.9
  187.1 0.3 broadcast_in_dim.19
  187.4 31.4 %all_to_all.45 = bf16[8,1024,128]{2,1,0:T(8,128)(2,1)S(1)} all-to-all(bf16[8,1024,128]{2,1,0:T(8,128)(2,1)S(1)} %broadcast_in_dim.19), channel_id=1, replica_groups=mesh['section'=4,'expert'=16,'tensor'=8] {'tensor'}, dimensions={0} | all-to-all | bytes 4194304 | tf_op jit(solution)/shard_map/all_to_all | solution.py:12
  218.8 1.4 copy.13
  220.2 2.3 dot_general.24
  222.5 3.4 %fusion = f32[4,256,640]{2,1,0:T(8,128)S(1)} fusion(bf16[4,256,1024]{2,1,0:T(8,128)(2,1)} %dot_general.24, bf16[1,1024,640]{2,1,0:T(8,128)(2,1)S(1)} %copy-done), kind=kOutput, calls=%fused_computation | convolution fusion | flops 1342177280 | bytes 6029312 | tf_op jit(solution)/shard_map/dot_general | solution.py:83
  225.9 36.1 %all_to_all.46 = f32[4,256,640]{2,1,0:T(8,128)} all-to-all(f32[4,256,640]{2,1,0:T(8,128)S(1)} %fusion), channel_id=1, replica_groups=mesh['section'=4,'expert'=16,'tensor'=8] {'section'}, dimensions={0} | all-to-all | bytes 5242880 | tf_op jit(solution)/shard_map/all_to_all | solution.py:39
  262.0 1.9 reduce_sum.62
  263.9 32.7 %all_to_all.47 = bf16[16,16,640]{2,1,0:T(8,128)(2,1)S(1)} all-to-all(bf16[16,16,640]{2,1,0:T(8,128)(2,1)S(1)} %bitcast.36), channel_id=1, replica_groups=mesh['section'=4,'expert'=16,'tensor'=8] {'expert'}, dimensions={0} | all-to-all | bytes 655360 | tf_op jit(solution)/shard_map/all_to_all | solution.py:85
  296.6 0.9 convolution_convert_fusion.1
  (13 shorter events, 0.2 us)
Async XLA Ops:
  6.5 216.0 %copy-start = (bf16[1,1024,640]{2,1,0:T(8,128)(2,1)S(1)}, bf16[1,1024,640]{2,1,0:T(8,128)(2,1)}, u32[]{:S(2)}) copy-start(bf16[1,1024,640]{2,1,0:T(8,128)(2,1)} %param.13) | copy-start | bytes 3932164
  8.3 11.5 %all-to-all-start = ((f32[8,128,1]{1,2,0:T(1,128)}), f32[8,128,1]{1,2,0:T(1,128)S(1)}, u32[]{:S(2)}, u32[]{:S(2)}) async-start(f32[8,128,1]{1,2,0:T(1,128)} %broadcast_in_dim.14), calls=%async_computation | async-start | bytes 8192 | tf_op jit(solution)/shard_map/all_to_all | solution.py:12
  21.6 9.6 %all-to-all-start.1 = ((f32[8,128,16]{1,2,0:T(8,128)}), f32[8,128,16]{1,2,0:T(8,128)S(1)}, u32[]{:S(2)}, u32[]{:S(2)}) async-start(f32[8,128,16]{1,2,0:T(8,128)} %broadcast_in_dim.15), calls=%async_computation.1 | async-start | bytes 131072 | tf_op jit(solution)/shard_map/all_to_all | solution.py:12
  25.0 151.8 %all-gather.2.cloned.1.call-start = ((), (), s32[]{:S(2)}) async-start(), calls=%async_computation.7 | async-start | bytes 13107200 | tf_op jit(solution)/shard_map/all_gather | solution.py:77
  94.2 82.6 %copy-start.2 = (bf16[1,5120,128]{2,1,0:T(8,128)(2,1)S(1)}, bf16[1,5120,128]{2,1,0:T(8,128)(2,1)}, u32[]{:S(2)}) copy-start(bf16[1,5120,128]{2,1,0:T(8,128)(2,1)} %param.11) | copy-start | bytes 3932164
  176.8 7.0 %copy-start.1 = (bf16[1024,5120]{0,1:T(8,128)(2,1)S(1)}, bf16[1024,5120]{0,1:T(8,128)(2,1)}, u32[]{:S(2)}) copy-start(bf16[1024,5120]{0,1:T(8,128)(2,1)} %all-gather.2.cloned.1.call-done) | copy-start | bytes 31457284
  176.8 7.3 %copy-start.3 = (bf16[1,5120,128]{2,1,0:T(8,128)(2,1)S(1)}, bf16[1,5120,128]{2,1,0:T(8,128)(2,1)}, u32[]{:S(2)}) copy-start(bf16[1,5120,128]{2,1,0:T(8,128)(2,1)} %param.12) | copy-start | bytes 3932164
Sparse Core Ops, SparseCore 0:
  94.4 82.4 all-gather.1
where the time goes:
time: 305 us; the launch traced here: 304 us
  blocking collectives  161 us (53%)
  waiting for transfers between devices  92.5 us (30%)
  matrix products  15.5 us (5%)
  between operations  13.5 us (4%)
  starting transfers between devices  8.79 us (3%)
  local copies, waits for them, and re-layouts  7.22 us (2%)
  other arithmetic  6.3 us (2%)
    all_gather x1, waiting for transfers between devices, on_device(): piece = lax.all_gather(widened, 'section', axis=0, tiled=True)  82.6 us
    all_to_all x2, blocking collectives, from_everyone(): lax.all_to_all(jnp.broadcast_to(array[None], (count, *array.shape)), axis...  59 us
    all_to_all x1, blocking collectives, summed_on_arrival(): lax.all_to_all(parts, axis, split_axis=0, concat_axis=0, tiled=True)  36.1 us
    all_to_all x1, blocking collectives, on_device(): lax.all_to_all(outgoing, 'expert', split_axis=0, concat_axis=0, tiled=True)  32.8 us
    all_to_all x1, blocking collectives, on_device(): lax.all_to_all(summed.astype(jnp.bfloat16), 'expert', split_axis=0, conca...  32.7 us
    all_to_all x2, waiting for transfers between devices, from_everyone(): lax.all_to_all(jnp.broadcast_to(array[None], (count, *array.shape)), axis...  9.89 us
    all_to_all x2, starting transfers between devices, from_everyone(): lax.all_to_all(jnp.broadcast_to(array[None], (count, *array.shape)), axis...  8.75 us
  transfers between devices with their start and end apart: 3, of which 3 were waited for; matrix products, arithmetic and copies ran while one was open for 1% of the time, Pallas kernels for 0%

commit v1 on v0

--- a/solution.py
+++ b/solution.py
@@ -74,7 +74,9 @@
     up_cols = up_proj[0]
     down_rows = down_proj[0]
     widened = collect(arrived, "tensor", 1)
-    piece = lax.all_gather(widened, "section", axis=0, tiled=True)
+    piece = jnp.concatenate(
+        lax.all_to_all(jnp.stack([widened] * lax.axis_size("section")), "section", 0, 0), axis=0
+    )
     gate = jnp.dot(piece, gate_cols, preferred_element_type=jnp.float32)
     upper = jnp.dot(piece, up_cols, preferred_element_type=jnp.float32)
     hidden = (jax.nn.silu(gate) * upper).astype(jnp.bfloat16)

time: 305 us -> 336 us (1.10)
  blocking collectives: 161 us -> 280 us
  waiting for transfers between devices: 92.5 us -> 9.94 us
  between operations: 13.5 us -> 0.11 us
  local copies, waits for them, and re-layouts: 7.22 us -> 17.2 us
    all_to_all x0 -> x1, blocking collectives: none -> 121 us  [on_device(): lax.all_to_all(jnp.stack([widened] * lax.axis_size('section')), 'section'...]
    all_gather x1 -> x0, waiting for transfers between devices: 82.6 us -> none  [on_device(): piece = lax.all_gather(widened, 'section', axis=0, tiled=True)]
    another operation x0 -> x2, local copies, waits for them, and re-layouts: none -> 11.5 us  [on_device(): jnp.stack([widened] * lax.axis_size('section'))]
  transfers between devices with their start and end apart: 3 -> 2, of which waited for: 3 -> 2; matrix products, arithmetic and copies ran while one was open for 1% -> 1% of each run, Pallas kernels for 0% -> 0%
where the time goes in v1:
time: 336 us; the launch traced here: 335 us
  blocking collectives  280 us (83%)
  local copies, waits for them, and re-layouts  17.2 us (5%)
  matrix products  12.5 us (4%)
  waiting for transfers between devices  9.94 us (3%)
  starting transfers between devices  8.75 us (3%)
  other arithmetic  6.3 us (2%)
    all_to_all x1, blocking collectives, on_device(): lax.all_to_all(jnp.stack([widened] * lax.axis_size('section')), 'section'...  121 us
    all_to_all x2, blocking collectives, from_everyone(): lax.all_to_all(jnp.broadcast_to(array[None], (count, *array.shape)), axis...  56.8 us
    all_to_all x1, blocking collectives, summed_on_arrival(): lax.all_to_all(parts, axis, split_axis=0, concat_axis=0, tiled=True)  36.1 us
    all_to_all x1, blocking collectives, on_device(): lax.all_to_all(outgoing, 'expert', split_axis=0, concat_axis=0, tiled=True)  32.8 us
    all_to_all x1, blocking collectives, on_device(): lax.all_to_all(summed.astype(jnp.bfloat16), 'expert', split_axis=0, conca...  32.8 us
    another operation x2, local copies, waits for them, and re-layouts, on_device(): jnp.stack([widened] * lax.axis_size('section'))  11.5 us
    all_to_all x2, waiting for transfers between devices, from_everyone(): lax.all_to_all(jnp.broadcast_to(array[None], (count, *array.shape)), axis...  9.94 us
    all_to_all x2, starting transfers between devices, from_everyone(): lax.all_to_all(jnp.broadcast_to(array[None], (count, *array.shape)), axis...  8.75 us
  transfers between devices with their start and end apart: 2, of which 2 were waited for; matrix products, arithmetic and copies ran while one was open for 1% of the time, Pallas kernels for 0%

profile of v1, /device:TPU:64, one launch (start us, length us, event | category | flops | bytes accessed | tf_op | source)
XLA Modules:
  0.0 334.8 jit_solution(1177243464983830592)
XLA Ops:
  0.0 1.1 fusion.12
  1.1 0.6 broadcast_in_dim.14
  1.7 5.4 %all-to-all-start = ((f32[8,128,1]{1,2,0:T(1,128)}), f32[8,128,1]{1,2,0:T(1,128)S(1)}, u32[]{:S(2)}, u32[]{:S(2)}) async-start(f32[8,128,1]{1,2,0:T(1,128)} %broadcast_in_dim.14), calls=%async_computation | async-start | bytes 8192 | tf_op jit(solution)/shard_map/all_to_all | solution.py:12
  7.1 0.7 fusion.18
  7.9 0.2 reduce_window_sum.11
  8.1 0.8 select_reduce_fusion.1
  8.9 4.3 %all-to-all-done = f32[8,128,1]{1,2,0:T(1,128)S(1)} async-done(((f32[8,128,1]{1,2,0:T(1,128)}), f32[8,128,1]{1,2,0:T(1,128)S(1)}, u32[]{:S(2)}, u32[]{:S(2)}) %all-to-all-start) | async-done | bytes 4128 | tf_op jit(solution)/shard_map/all_to_all | solution.py:12
  13.3 1.1 fusion.19
  14.4 0.7 broadcast_in_dim.15
  15.1 3.4 %all-to-all-start.1 = ((f32[8,128,16]{1,2,0:T(8,128)}), f32[8,128,16]{1,2,0:T(8,128)S(1)}, u32[]{:S(2)}, u32[]{:S(2)}) async-start(f32[8,128,16]{1,2,0:T(8,128)} %broadcast_in_dim.15), calls=%async_computation.1 | async-start | bytes 131072 | tf_op jit(solution)/shard_map/all_to_all | solution.py:12
  18.4 0.7 fusion.22
  19.1 5.6 %all-to-all-done.1 = f32[8,128,16]{1,2,0:T(8,128)S(1)} async-done(((f32[8,128,16]{1,2,0:T(8,128)}), f32[8,128,16]{1,2,0:T(8,128)S(1)}, u32[]{:S(2)}, u32[]{:S(2)}) %all-to-all-start.1) | async-done | bytes 65568 | tf_op jit(solution)/shard_map/all_to_all | solution.py:12
  24.8 0.8 select_reduce_fusion
  25.7 1.3 convolution_convert_fusion
  27.0 32.8 %all_to_all.48 = bf16[16,16,640]{2,1,0:T(8,128)(2,1)S(1)} all-to-all(bf16[16,16,640]{2,1,0:T(8,128)(2,1)S(1)} %bitcast.40), channel_id=1, replica_groups=mesh['section'=4,'expert'=16,'tensor'=8] {'expert'}, dimensions={0} | all-to-all | bytes 655360 | tf_op jit(solution)/shard_map/all_to_all | solution.py:72
  59.8 0.2 copy.14
  60.0 0.2 broadcast_in_dim.18
  60.1 27.5 %all_to_all.49 = bf16[8,256,640]{1,2,0:T(8,128)(2,1)} all-to-all(bf16[8,256,640]{1,2,0:T(8,128)(2,1)S(1)} %broadcast_in_dim.18), channel_id=1, replica_groups=mesh['section'=4,'expert'=16,'tensor'=8] {'tensor'}, dimensions={0} | all-to-all | bytes 5242880 | tf_op jit(solution)/shard_map/all_to_all | solution.py:12
  87.7 4.5 %copy.15 = bf16[256,5120]{1,0:T(8,128)(2,1)} copy(bf16[256,5120]{0,1:T(8,128)(2,1)} %bitcast.37) | data formatting | bytes 5242880 | tf_op jit(solution)/shard_map/stack;reshape | solution.py:78
  92.1 7.0 %stack.3 = bf16[4,256,5120]{2,1,0:T(8,128)(2,1)} broadcast(bf16[256,5120]{1,0:T(8,128)(2,1)} %copy.15), dimensions={1,2} | broadcast | bytes 13107200 | tf_op jit(solution)/shard_map/stack | solution.py:78
  99.2 121.5 %all_to_all.50 = bf16[4,256,5120]{2,1,0:T(8,128)(2,1)S(1)} all-to-all(bf16[4,256,5120]{2,1,0:T(8,128)(2,1)} %stack.3), channel_id=1, replica_groups=mesh['section'=4,'expert'=16,'tensor'=8] {'section'}, dimensions={0} | all-to-all | bytes 20971520 | tf_op jit(solution)/shard_map/all_to_all | solution.py:78
  220.7 2.9 fusion.4
  223.6 2.9 fusion.9
  226.4 0.3 broadcast_in_dim.19
  226.7 29.3 %all_to_all.51 = bf16[8,1024,128]{2,1,0:T(8,128)(2,1)S(1)} all-to-all(bf16[8,1024,128]{2,1,0:T(8,128)(2,1)S(1)} %broadcast_in_dim.19), channel_id=1, replica_groups=mesh['section'=4,'expert'=16,'tensor'=8] {'tensor'}, dimensions={0} | all-to-all | bytes 4194304 | tf_op jit(solution)/shard_map/all_to_all | solution.py:12
  256.0 1.4 copy.16
  257.4 2.3 dot_general.24
  259.7 3.4 %fusion = f32[4,256,640]{2,1,0:T(8,128)S(1)} fusion(bf16[4,256,1024]{2,1,0:T(8,128)(2,1)} %dot_general.24, bf16[1,1024,640]{2,1,0:T(8,128)(2,1)S(1)} %copy-done), kind=kOutput, calls=%fused_computation | convolution fusion | flops 1342177280 | bytes 6029312 | tf_op jit(solution)/shard_map/dot_general | solution.py:85
  263.1 36.1 %all_to_all.52 = f32[4,256,640]{2,1,0:T(8,128)} all-to-all(f32[4,256,640]{2,1,0:T(8,128)S(1)} %fusion), channel_id=1, replica_groups=mesh['section'=4,'expert'=16,'tensor'=8] {'section'}, dimensions={0} | all-to-all | bytes 5242880 | tf_op jit(solution)/shard_map/all_to_all | solution.py:39
  299.2 1.9 reduce_sum.62
  301.1 32.8 %all_to_all.53 = bf16[16,16,640]{2,1,0:T(8,128)(2,1)S(1)} all-to-all(bf16[16,16,640]{2,1,0:T(8,128)(2,1)S(1)} %bitcast.39), channel_id=1, replica_groups=mesh['section'=4,'expert'=16,'tensor'=8] {'expert'}, dimensions={0} | all-to-all | bytes 655360 | tf_op jit(solution)/shard_map/all_to_all | solution.py:87
  333.8 0.9 convolution_convert_fusion.1
  (11 shorter events, 0.2 us)
Async XLA Ops:
  0.0 259.7 %copy-start = (bf16[1,1024,640]{2,1,0:T(8,128)(2,1)S(1)}, bf16[1,1024,640]{2,1,0:T(8,128)(2,1)}, u32[]{:S(2)}) copy-start(bf16[1,1024,640]{2,1,0:T(8,128)(2,1)} %param.13) | copy-start | bytes 3932164
  1.7 11.5 %all-to-all-start = ((f32[8,128,1]{1,2,0:T(1,128)}), f32[8,128,1]{1,2,0:T(1,128)S(1)}, u32[]{:S(2)}, u32[]{:S(2)}) async-start(f32[8,128,1]{1,2,0:T(1,128)} %broadcast_in_dim.14), calls=%async_computation | async-start | bytes 8192 | tf_op jit(solution)/shard_map/all_to_all | solution.py:12
  15.1 9.6 %all-to-all-start.1 = ((f32[8,128,16]{1,2,0:T(8,128)}), f32[8,128,16]{1,2,0:T(8,128)S(1)}, u32[]{:S(2)}, u32[]{:S(2)}) async-start(f32[8,128,16]{1,2,0:T(8,128)} %broadcast_in_dim.15), calls=%async_computation.1 | async-start | bytes 131072 | tf_op jit(solution)/shard_map/all_to_all | solution.py:12
  99.2 121.5 %copy-start.1 = (bf16[1,5120,128]{2,1,0:T(8,128)(2,1)S(1)}, bf16[1,5120,128]{2,1,0:T(8,128)(2,1)}, u32[]{:S(2)}) copy-start(bf16[1,5120,128]{2,1,0:T(8,128)(2,1)} %param.11) | copy-start | bytes 3932164
  220.7 2.9 copy-start.2
